TPU v7x, 32 devices: a whole 2x2x4 slice. The times are simulated.
32 devices in a mesh: stream: 2 (over x), span: 4 (over y, core), depth: 4 (over z).
Axes of the slice: x: 2, y: 2, z: 4, core: 2. Of those that a mesh axis runs over, the one named last changes fastest.
Arguments:
- forward_velocity: float32 [3, 16, 64, 512], P(None, 'stream', 'span', 'depth'), may hold values from -40 to 40, as said below
- adjoint_velocity: float32 [3, 16, 64, 512], P(None, 'stream', 'span', 'depth'), may hold values from -40 to 40, as said below
- weights: float32 [32, 81], replicated, may hold values from -0.625 to 0.625
Outputs:
- basis: float32 [32, 16, 64, 512], P(None, 'stream', 'span', 'depth')
Inputs may be any that keep to these rules, and one draw needn't show every extreme that they name: `forward_velocity`: a velocity field whose amplitude varies from cell to cell. `adjoint_velocity`: a velocity field whose amplitude varies from cell to cell.
All inputs are finite; a program needn't handle non-finite values.
Results may differ from a plain program's by a relative error of at most 0.0003.
Values sent between devices are 32-bit elements; how exact they have to be, the bound alone decides.
A program may use at most 64 MiB of HBM per device.

v0:
```python
import functools

import jax
import jax.numpy as jnp
from jax import lax
from jax.experimental import pallas as pl
from jax.experimental.pallas import tpu as pltpu
from jax.sharding import PartitionSpec as P

MESH = pl.DeviceIdType.MESH
F32 = jnp.float32
BF16 = jnp.bfloat16
AXES = ("stream", "span", "depth")
HBM = pl.BlockSpec(memory_space=pltpu.HBM)
VMEM = pl.BlockSpec(memory_space=pltpu.VMEM)
LIMIT = 48 * 1024 * 1024


def split(value):
    high = value.astype(BF16)
    low = (value - high.astype(F32)).astype(BF16)
    return high, low


def snap_kernel(sizes, f_ref, a_ref, w_ref, s_ref, t_ref, px, py, hy, hz, ysend, zsend, wv, gs, sx, sz, lhs, acc,
                one, two, local, send, recv, send1, recv1, send2, recv2):
    n_s, n_y, n_z = sizes
    i_s, i_y, i_z = [lax.axis_index(name) for name in AXES]
    count = n_s * n_y
    me = i_s * n_y + i_y
    planes, rows = f_ref.shape[1], f_ref.shape[2]
    half = 3 * planes
    cells = rows * 128
    tall = rows + 16

    def plane_peer(k):
        other = lax.rem(me + k, count)
        return {"stream": other // n_y, "span": lax.rem(other, n_y)}

    def depth_peer(k):
        return {"depth": lax.rem(i_z + k, n_z)}

    barrier = pltpu.get_barrier_semaphore()
    for k in range(1, count):
        pl.semaphore_signal(barrier, inc=1, device_id=plane_peer(k), device_id_type=MESH)
    for k in range(1, n_z):
        pl.semaphore_signal(barrier, inc=1, device_id=depth_peer(k), device_id_type=MESH)

    loads = []

    def load(src, dst):
        copy = pltpu.make_async_copy(src, dst, local.at[len(loads)])
        copy.start()
        loads.append(copy)

    for k, ref in enumerate((f_ref, a_ref)):
        for c in range(3):
            m = 3 * k + c
            load(ref.at[c], py.at[m * planes:(m + 1) * planes, 8:8 + rows])
        load(ref, px.at[3 * k:3 * k + 3, 2:planes + 2])
    load(w_ref, wv)
    pl.semaphore_wait(barrier, count - 1 + n_z - 1)
    copies = []

    def push(src, dst, peer):
        n = len(copies)
        copy = pltpu.make_async_remote_copy(
            src_ref=src, dst_ref=dst, send_sem=send.at[n], recv_sem=recv.at[n],
            device_id=peer, device_id_type=MESH)
        copy.start()
        copies.append(copy)

    def sides(name, size, mine):
        return {name: lax.rem(mine + 1, size)}, {name: lax.rem(mine + size - 1, size)}

    after_x, before_x = sides("stream", n_s, i_s)
    after_y, before_y = sides("span", n_y, i_y)
    after_z, before_z = sides("depth", n_z, i_z)
    for k, ref in enumerate((f_ref, a_ref)):
        push(ref.at[:, planes - 2:planes], px.at[3 * k:3 * k + 3, 0:2], after_x)
    for k, ref in enumerate((f_ref, a_ref)):
        push(ref.at[:, 0:2], px.at[3 * k:3 * k + 3, planes + 2:planes + 4], before_x)

    for copy in loads:
        copy.wait()
    flat = py.reshape(2 * half * tall, 128)
    for j in range(2):
        ysend[0, j] = flat[pl.ds(6 + rows + j, 2 * half, stride=tall), :]
        ysend[1, j] = flat[pl.ds(8 + j, 2 * half, stride=tall), :]
    lane = lax.broadcasted_iota(jnp.int32, (rows, 128), 1)
    for k in range(2):
        last = jnp.zeros((rows, 128), F32)
        first = jnp.zeros((rows, 128), F32)
        for i in range(half):
            own = py[k * half + i, 8:8 + rows, :]
            head = jnp.where(lane == 0, -own, 8.0 * pltpu.roll(own, 1, 1) - own)
            tail = jnp.where(lane == 126, own - 8.0 * pltpu.roll(own, 127, 1), own)
            head = pltpu.roll(head, 4 * i, 1) if i else head
            tail = pltpu.roll(tail, (4 * i + 4) % 128, 1)
            first = jnp.where(lane // 4 == i, head, first)
            last = jnp.where(lane // 4 == i, tail, last)
        zsend[0, k] = last
        zsend[1, k] = first

    push(ysend.at[0], hy.at[0], after_y)
    push(ysend.at[1], hy.at[1], before_y)
    push(zsend.at[0], hz.at[0], after_z)
    push(zsend.at[1], hz.at[1], before_z)

    row = lax.broadcasted_iota(jnp.int32, (81, 176), 0)
    col = lax.broadcasted_iota(jnp.int32, (81, 176), 1)
    block, r = col // 16, col % 8
    source = jnp.where(block < 9, block * 9 + r, jnp.where(block == 9, r * 9 + 8, 80))
    keep = (row == source) & ((block < 10) | (r == 0))
    pick = jnp.where(keep, 1.0, 0.0).astype(BF16)
    w_high, w_low = split(wv[...] * (1.0 / 144.0))
    lhs[0:32, :] = jnp.dot(w_high, pick, preferred_element_type=F32).astype(BF16)
    lhs[32:64, :] = jnp.dot(w_low, pick, preferred_element_type=F32).astype(BF16)
    acc[...] = jnp.zeros_like(acc)

    def stencil(m2, m1, p1, p2):
        return 8.0 * (p1 - m1) - (p2 - m2)

    @pl.loop(0, planes)
    def _(x):
        for m in range(6):
            own = px[m, x + 2]
            p1 = jnp.where(lane == 127, 0.0, pltpu.roll(own, 127, 1))
            p2 = jnp.where(lane >= 126, 0.0, pltpu.roll(own, 126, 1))
            m1 = jnp.where(lane == 0, 0.0, pltpu.roll(own, 1, 1))
            m2 = jnp.where(lane <= 1, 0.0, pltpu.roll(own, 2, 1))
            sz[m * planes + x] = stencil(m2, m1, p1, p2)

    @pl.loop(2, planes - 2)
    def _(x):
        for m in range(6):
            sx[m * planes + x] = stencil(px[m, x], px[m, x + 1], px[m, x + 3], px[m, x + 4])

    for copy in copies[4:8]:
        copy.wait()
    for j in range(2):
        flat[pl.ds(6 + j, 2 * half, stride=tall), :] = hy[0, j]
        flat[pl.ds(8 + rows + j, 2 * half, stride=tall), :] = hy[1, j]

    def inner_x(x, k, c):
        m = 3 * k + c
        return stencil(px[m, x], px[m, x + 1], px[m, x + 3], px[m, x + 4])

    def plane(x, slot, ready):
        for k in range(2):
            halo_z = jnp.where(lane % 4 < 2, hz[1, k], hz[0, k])
            for c in range(3):
                i = (3 * k + c) * planes + x
                dx = sx[i] if ready else inner_x(x, k, c)
                dy = stencil(*[py[i, 8 + o:8 + o + rows, :] for o in (-2, -1, 1, 2)])
                edge = pltpu.roll(halo_z, lax.rem(254 - 4 * (c * planes + x), 128), 1)
                dz = sz[i] + jnp.where((lane < 2) | (lane >= 126), edge, 0.0)
                for d, slope in enumerate((dx, dy, dz)):
                    gs[slot, pl.ds(16 * k + 3 * c + d, rows, stride=32), :] = slope
        parts = []
        for pair in range(0, rows, 2):
            tiles = []
            for y in (pair, pair + 1):
                base = 32 * y
                f8 = gs[slot, base:base + 8, :]
                a8 = gs[slot, base + 16:base + 24, :]
                a_end = gs[slot, base + 24:base + 25, :]
                blocks = []
                for n in range(11):
                    if n < 9:
                        part = gs[slot, base + n:base + n + 1, :] * a8
                    elif n == 9:
                        part = f8 * a_end
                    else:
                        part = jnp.broadcast_to(gs[slot, base + 8:base + 9, :] * a_end, (8, 128))
                    high = part.astype(BF16).astype(F32)
                    blocks.append(jnp.concatenate([high, part - high], axis=0).astype(BF16))
                tiles.append(jnp.concatenate(blocks, axis=0))
            wide = jnp.dot(lhs[...], jnp.concatenate(tiles, axis=1), preferred_element_type=F32)
            high, low = split(wide[:32] + wide[32:])
            both = jnp.concatenate([high, low], axis=0)
            s_ref[:, pl.ds(pl.multiple_of(x * cells + pair * 128, 256), 256)] = both
            parts.append(both)
        both = jnp.concatenate(parts, axis=1)
        acc[...] += lax.dot_general(both, both, (((1,), (1,)), ((), ())), preferred_element_type=F32)

    @pl.loop(2, planes - 2, step=2)
    def _(x):
        plane(x, 0, True)
        plane(x + 1, 1, True)

    for copy in copies[0:2]:
        copy.wait()
    plane(0, 0, False)
    plane(1, 1, False)
    for copy in copies[2:4]:
        copy.wait()
    plane(planes - 2, 0, False)
    plane(planes - 1, 1, False)

    total = acc[0:32, :] + acc[32:64, :]
    gram = total[:, :32] + total[:, 32:]
    one[me] = jnp.concatenate([gram[8 * q:8 * q + 8, :] for q in range(4)], axis=1)

    def exchange(buf, mine, number, peer_of, send, recv):
        moves = []
        for k in range(1, number):
            copy = pltpu.make_async_remote_copy(
                src_ref=buf.at[mine], dst_ref=buf.at[mine], send_sem=send.at[k], recv_sem=recv.at[k],
                device_id=peer_of(k), device_id_type=MESH)
            copy.start()
            moves.append(copy)
        for copy in moves:
            copy.wait()
        total = buf[0]
        for k in range(1, number):
            total = total + buf[k]
        return total

    two[i_z] = exchange(one, me, count, plane_peer, send1, recv1)
    t_ref[...] = exchange(two, i_z, n_z, depth_peer, send2, recv2)


def factor(gram):
    lane = lax.broadcasted_iota(jnp.int32, (32, 128), 1)
    row = lax.broadcasted_iota(jnp.int32, (32, 128), 0)
    work = jnp.where(lane < 32, gram, jnp.where(lane - 32 == row, 1.0, 0.0))
    scale = jnp.zeros((32, 128), F32)
    for base in range(0, 32, 8):
        cols = [jnp.broadcast_to(work[:, base + q:base + q + 1], (32, 128)) for q in range(8)]
        for q in range(8):
            j = base + q
            pivot = jnp.broadcast_to(cols[q][j:j + 1, :], (32, 128))
            ratio = jnp.where(row > j, cols[q] * (1.0 / pivot), 0.0)
            for t in range(q + 1, 8):
                cols[t] = cols[t] - ratio * cols[t][j:j + 1, :]
            work = work - ratio * work[j:j + 1, :]
            scale = jnp.where(row == j, pivot, scale)
    return pltpu.roll(work, 96, 1) * lax.rsqrt(scale)


def basis_kernel(cells, planes, t_ref, s_ref, o_ref, stage, sems):
    width = s_ref.shape[1] // planes
    packed = t_ref[...] * (1.0 / cells)
    gram = jnp.concatenate([packed if q == 0 else pltpu.roll(packed, 128 - 32 * q, 1) for q in range(4)], axis=0)
    inverse = factor(gram)[:, :32]
    high, low = split(inverse)
    left = jnp.concatenate(
        [jnp.concatenate([high, high], axis=1), jnp.concatenate([low, low], axis=1)], axis=0)
    rows = o_ref.shape[2]
    flat = stage.reshape(32 * planes * rows, 128)
    copies = []
    for x in range(planes):
        wide = jnp.dot(left, s_ref[:, x * width:(x + 1) * width], preferred_element_type=F32)
        block = wide[:32] + wide[32:]
        for y in range(rows):
            flat[pl.ds(x * rows + y, 32, stride=planes * rows), :] = block[:, 128 * y:128 * y + 128]
        copy = pltpu.make_async_copy(stage.at[:, pl.ds(x * rows, rows), :], o_ref.at[:, x], sems.at[x])
        copy.start()
        copies.append(copy)
    for copy in copies:
        copy.wait()


def body(sizes, forward, adjoint, weights):
    _, planes, rows, depth = forward.shape
    half = 3 * planes
    plane_count = sizes[0] * sizes[1]
    cells = planes * rows * depth * plane_count * sizes[2]
    total, snaps = pl.pallas_call(
        functools.partial(snap_kernel, sizes),
        out_shape=(
            jax.ShapeDtypeStruct((64, planes * rows * depth), BF16),
            jax.ShapeDtypeStruct((8, 128), F32)),
        in_specs=[HBM] * 3,
        out_specs=(VMEM, VMEM),
        scratch_shapes=[
            pltpu.VMEM((6, planes + 4, rows, depth), F32),
            pltpu.VMEM((2 * half, rows + 16, depth), F32),
            pltpu.VMEM((2, 2, 2 * half, depth), F32),
            pltpu.VMEM((2, 2, rows, depth), F32),
            pltpu.VMEM((2, 2, 2 * half, depth), F32),
            pltpu.VMEM((2, 2, rows, depth), F32),
            pltpu.VMEM((32, 81), F32),
            pltpu.VMEM((2, rows * 32, depth), F32),
            pltpu.VMEM((2 * half, rows, depth), F32),
            pltpu.VMEM((2 * half, rows, depth), F32),
            pltpu.VMEM((64, 176), BF16),
            pltpu.VMEM((64, 64), F32),
            pltpu.VMEM((plane_count, 8, 128), F32),
            pltpu.VMEM((sizes[2], 8, 128), F32),
            pltpu.SemaphoreType.DMA((9,)),
            pltpu.SemaphoreType.DMA((8,)),
            pltpu.SemaphoreType.DMA((8,)),
            pltpu.SemaphoreType.DMA((plane_count,)),
            pltpu.SemaphoreType.DMA((plane_count,)),
            pltpu.SemaphoreType.DMA((sizes[2],)),
            pltpu.SemaphoreType.DMA((sizes[2],))],
        compiler_params=pltpu.CompilerParams(collective_id=0, has_side_effects=True, vmem_limit_bytes=LIMIT),
        name="snap",
    )(*[pltpu.with_memory_space_constraint(value, pltpu.HBM) for value in (forward, adjoint, weights)])[::-1]
    return pl.pallas_call(
        functools.partial(basis_kernel, cells, planes),
        out_shape=jax.ShapeDtypeStruct((32, planes, rows, depth), F32),
        in_specs=[VMEM, VMEM],
        out_specs=HBM,
        scratch_shapes=[
            pltpu.VMEM((32, planes * rows, depth), F32),
            pltpu.SemaphoreType.DMA((planes,))],
        compiler_params=pltpu.CompilerParams(vmem_limit_bytes=LIMIT),
        name="basis",
    )(total, snaps)


def solution(mesh):
    sizes = tuple(mesh.shape[name] for name in AXES)
    in_specs = (P(None, *AXES), P(None, *AXES), P())
    return jax.shard_map(
        functools.partial(body, sizes), mesh=mesh, in_specs=in_specs, out_specs=P(None, *AXES), check_vma=False)
```

profile of v0, /device:TPU:0, one launch (start us, length us, event | category | flops | bytes accessed | tf_op | source)
XLA Modules:
  0.0 25.4 jit_solution(14451139915615603347)
XLA Ops:
  0.0 22.1 %snap.1 = (bf16[64,16384]{1,0:T(8,128)(2,1)S(1)}, f32[8,128]{1,0:T(8,128)S(1)}) custom-call(f32[3,8,16,128]{3,2,1,0:T(8,128)} %f_ref.1, f32[3,8,16,128]{3,2,1,0:T(8,128)} %a_ref.1, f32[32,81]{1,0:T(8,128)} %w_ref.1), custom_call_target="tpu_custom_call" | custom-call | tf_op jit(solution)/shard_map/snap/pallas_call | solution.py:270
  22.1 3.3 %basis.1 = f32[32,8,16,128]{3,2,1,0:T(8,128)} custom-call(f32[8,128]{1,0:T(8,128)S(1)} %get-tuple-element.7.t_ref, bf16[64,16384]{1,0:T(8,128)(2,1)S(1)} %get-tuple-element.8.s_ref), custom_call_target="tpu_custom_call" | custom-call | tf_op jit(solution)/shard_map/basis/pallas_call | solution.py:302
where the time goes:
time: 25.5 us; the launch traced here: 25.4 us
  Pallas kernels  25.4 us (100%)
    pallas_call x1, Pallas kernels, body(): pl.pallas_call(functools.partial(snap_kernel, sizes), out_shape=(jax.Shap...  22.1 us
    pallas_call x1, Pallas kernels, body(): pl.pallas_call(functools.partial(basis_kernel, cells, planes), out_shape=...  3.29 us

commit v1 on v0

--- a/solution.py
+++ b/solution.py
@@ -78,8 +78,6 @@
     after_z, before_z = sides("depth", n_z, i_z)
     for k, ref in enumerate((f_ref, a_ref)):
         push(ref.at[:, planes - 2:planes], px.at[3 * k:3 * k + 3, 0:2], after_x)
-    for k, ref in enumerate((f_ref, a_ref)):
-        push(ref.at[:, 0:2], px.at[3 * k:3 * k + 3, planes + 2:planes + 4], before_x)
 
     for copy in loads:
         copy.wait()
@@ -106,6 +104,8 @@
     push(ysend.at[1], hy.at[1], before_y)
     push(zsend.at[0], hz.at[0], after_z)
     push(zsend.at[1], hz.at[1], before_z)
+    for k, ref in enumerate((f_ref, a_ref)):
+        push(ref.at[:, 0:2], px.at[3 * k:3 * k + 3, planes + 2:planes + 4], before_x)
 
     row = lax.broadcasted_iota(jnp.int32, (81, 176), 0)
     col = lax.broadcasted_iota(jnp.int32, (81, 176), 1)
@@ -136,7 +136,7 @@
         for m in range(6):
             sx[m * planes + x] = stencil(px[m, x], px[m, x + 1], px[m, x + 3], px[m, x + 4])
 
-    for copy in copies[4:8]:
+    for copy in copies[2:6]:
         copy.wait()
     for j in range(2):
         flat[pl.ds(6 + j, 2 * half, stride=tall), :] = hy[0, j]
@@ -193,7 +193,7 @@
         copy.wait()
     plane(0, 0, False)
     plane(1, 1, False)
-    for copy in copies[2:4]:
+    for copy in copies[6:8]:
         copy.wait()
     plane(planes - 2, 0, False)
     plane(planes - 1, 1, False)
@@ -222,21 +222,32 @@
 
 
 def factor(gram):
-    lane = lax.broadcasted_iota(jnp.int32, (32, 128), 1)
-    row = lax.broadcasted_iota(jnp.int32, (32, 128), 0)
-    work = jnp.where(lane < 32, gram, jnp.where(lane - 32 == row, 1.0, 0.0))
-    scale = jnp.zeros((32, 128), F32)
-    for base in range(0, 32, 8):
-        cols = [jnp.broadcast_to(work[:, base + q:base + q + 1], (32, 128)) for q in range(8)]
+    lane = lax.broadcasted_iota(jnp.int32, (8, 128), 1)
+    row = lax.broadcasted_iota(jnp.int32, (8, 128), 0)
+    work = [
+        jnp.where(lane < 32, gram[8 * b:8 * b + 8, :], jnp.where(lane - 32 == row + 8 * b, 1.0, 0.0))
+        for b in range(4)]
+    done = []
+    for top in range(4):
+        cols = [
+            [jnp.broadcast_to(work[b][:, 8 * top + q:8 * top + q + 1], (8, 128)) for b in range(top, 4)]
+            for q in range(8)]
+        scale = jnp.zeros((8, 128), F32)
         for q in range(8):
-            j = base + q
-            pivot = jnp.broadcast_to(cols[q][j:j + 1, :], (32, 128))
-            ratio = jnp.where(row > j, cols[q] * (1.0 / pivot), 0.0)
-            for t in range(q + 1, 8):
-                cols[t] = cols[t] - ratio * cols[t][j:j + 1, :]
-            work = work - ratio * work[j:j + 1, :]
-            scale = jnp.where(row == j, pivot, scale)
-    return pltpu.roll(work, 96, 1) * lax.rsqrt(scale)
+            pivot = cols[q][0][q:q + 1, :]
+            inverse = 1.0 / pivot
+            scale = jnp.where(row == q, pivot, scale)
+            heads = [cols[t][0][q:q + 1, :] for t in range(q + 1, 8)]
+            lead = work[top][q:q + 1, :]
+            for b in range(top, 4):
+                ratio = cols[q][b - top] * inverse
+                if b == top:
+                    ratio = jnp.where(row > q, ratio, 0.0)
+                for t, head in zip(range(q + 1, 8), heads):
+                    cols[t][b - top] = cols[t][b - top] - ratio * head
+                work[b] = work[b] - ratio * lead
+        done.append(pltpu.roll(work[top], 96, 1) * lax.rsqrt(scale))
+    return jnp.concatenate(done, axis=0)
 
 
 def basis_kernel(cells, planes, t_ref, s_ref, o_ref, stage, sems):

time: 25.5 us -> 25.4 us (level)
  no operation moved by 1% of the time
where the time goes in v1:
time: 25.4 us; the launch traced here: 25.2 us
  Pallas kernels  25.2 us (99%)
    pallas_call x1, Pallas kernels, body(): pl.pallas_call(functools.partial(snap_kernel, sizes), out_shape=(jax.Shap...  22 us
    pallas_call x1, Pallas kernels, body(): pl.pallas_call(functools.partial(basis_kernel, cells, planes), out_shape=...  3.28 us

profile of v1, /device:TPU:0, one launch (start us, length us, event | category | flops | bytes accessed | tf_op | source)
XLA Modules:
  0.0 25.2 jit_solution(5018529395889689634)
XLA Ops:
  0.0 22.0 %snap.1 = (bf16[64,16384]{1,0:T(8,128)(2,1)S(1)}, f32[8,128]{1,0:T(8,128)S(1)}) custom-call(f32[3,8,16,128]{3,2,1,0:T(8,128)} %f_ref.1, f32[3,8,16,128]{3,2,1,0:T(8,128)} %a_ref.1, f32[32,81]{1,0:T(8,128)} %w_ref.1), custom_call_target="tpu_custom_call" | custom-call | tf_op jit(solution)/shard_map/snap/pallas_call | solution.py:281
  22.0 3.3 %basis.1 = f32[32,8,16,128]{3,2,1,0:T(8,128)} custom-call(f32[8,128]{1,0:T(8,128)S(1)} %get-tuple-element.7.t_ref, bf16[64,16384]{1,0:T(8,128)(2,1)S(1)} %get-tuple-element.8.s_ref), custom_call_target="tpu_custom_call" | custom-call | tf_op jit(solution)/shard_map/basis/pallas_call | solution.py:313

commit v2 on v1

--- a/solution.py
+++ b/solution.py
@@ -41,10 +41,14 @@
         return {"depth": lax.rem(i_z + k, n_z)}
 
     barrier = pltpu.get_barrier_semaphore()
-    for k in range(1, count):
-        pl.semaphore_signal(barrier, inc=1, device_id=plane_peer(k), device_id_type=MESH)
-    for k in range(1, n_z):
-        pl.semaphore_signal(barrier, inc=1, device_id=depth_peer(k), device_id_type=MESH)
+    direct = count * n_z <= 32
+    greeted = 0
+    for z in range(n_z):
+        for k in range(count):
+            if (k or z) and (direct or not k or not z):
+                peer = {**plane_peer(k), **depth_peer(z)}
+                pl.semaphore_signal(barrier, inc=1, device_id=peer, device_id_type=MESH)
+                greeted += 1
 
     loads = []
 
@@ -59,7 +63,7 @@
             load(ref.at[c], py.at[m * planes:(m + 1) * planes, 8:8 + rows])
         load(ref, px.at[3 * k:3 * k + 3, 2:planes + 2])
     load(w_ref, wv)
-    pl.semaphore_wait(barrier, count - 1 + n_z - 1)
+    pl.semaphore_wait(barrier, greeted)
     copies = []
 
     def push(src, dst, peer):
@@ -200,7 +204,7 @@
 
     total = acc[0:32, :] + acc[32:64, :]
     gram = total[:, :32] + total[:, 32:]
-    one[me] = jnp.concatenate([gram[8 * q:8 * q + 8, :] for q in range(4)], axis=1)
+    packed = jnp.concatenate([gram[8 * q:8 * q + 8, :] for q in range(4)], axis=1)
 
     def exchange(buf, mine, number, peer_of, send, recv):
         moves = []
@@ -217,8 +221,30 @@
             total = total + buf[k]
         return total
 
-    two[i_z] = exchange(one, me, count, plane_peer, send1, recv1)
-    t_ref[...] = exchange(two, i_z, n_z, depth_peer, send2, recv2)
+    if not direct:
+        one[me] = packed
+        two[i_z] = exchange(one, me, count, plane_peer, send1, recv1)
+        t_ref[...] = exchange(two, i_z, n_z, depth_peer, send2, recv2)
+        return
+    everyone = me * n_z + i_z
+    one[everyone] = packed
+    moves = []
+    for z in (*range(1, n_z), 0):
+        for k in range(count - 1, -1, -1):
+            if k == 0 and z == 0:
+                continue
+            slot = z * count + k
+            copy = pltpu.make_async_remote_copy(
+                src_ref=one.at[everyone], dst_ref=one.at[everyone], send_sem=send1.at[slot],
+                recv_sem=recv1.at[slot], device_id={**plane_peer(k), **depth_peer(z)}, device_id_type=MESH)
+            copy.start()
+            moves.append(copy)
+    for copy in moves:
+        copy.wait()
+    sums = [one[k] for k in range(count * n_z)]
+    while len(sums) > 1:
+        sums = [x + y for x, y in zip(sums[::2], sums[1::2])] + sums[len(sums) - len(sums) % 2:]
+    t_ref[...] = sums[0]
 
 
 def factor(gram):
@@ -267,7 +293,7 @@
         for y in range(rows):
             flat[pl.ds(x * rows + y, 32, stride=planes * rows), :] = block[:, 128 * y:128 * y + 128]
         copy = pltpu.make_async_copy(stage.at[:, pl.ds(x * rows, rows), :], o_ref.at[:, x], sems.at[x])
-        copy.start()
+        copy.start(priority=x % 2)
         copies.append(copy)
     for copy in copies:
         copy.wait()
@@ -277,6 +303,7 @@
     _, planes, rows, depth = forward.shape
     half = 3 * planes
     plane_count = sizes[0] * sizes[1]
+    slots = plane_count * sizes[2] if plane_count * sizes[2] <= 32 else plane_count
     cells = planes * rows * depth * plane_count * sizes[2]
     total, snaps = pl.pallas_call(
         functools.partial(snap_kernel, sizes),
@@ -298,13 +325,13 @@
             pltpu.VMEM((2 * half, rows, depth), F32),
             pltpu.VMEM((64, 176), BF16),
             pltpu.VMEM((64, 64), F32),
-            pltpu.VMEM((plane_count, 8, 128), F32),
+            pltpu.VMEM((slots, 8, 128), F32),
             pltpu.VMEM((sizes[2], 8, 128), F32),
             pltpu.SemaphoreType.DMA((9,)),
             pltpu.SemaphoreType.DMA((8,)),
             pltpu.SemaphoreType.DMA((8,)),
-            pltpu.SemaphoreType.DMA((plane_count,)),
-            pltpu.SemaphoreType.DMA((plane_count,)),
+            pltpu.SemaphoreType.DMA((slots,)),
+            pltpu.SemaphoreType.DMA((slots,)),
             pltpu.SemaphoreType.DMA((sizes[2],)),
             pltpu.SemaphoreType.DMA((sizes[2],))],
         compiler_params=pltpu.CompilerParams(collective_id=0, has_side_effects=True, vmem_limit_bytes=LIMIT),

time: 25.4 us -> 24 us (0.945)
  Pallas kernels: 25.2 us -> 23.9 us
    pallas_call x1, Pallas kernels: 22 us -> 20.6 us  [body(): pl.pallas_call(functools.partial(snap_kernel, sizes), out_shape=(jax.Shap...]
where the time goes in v2:
time: 24 us; the launch traced here: 23.9 us
  Pallas kernels  23.9 us (100%)
    pallas_call x1, Pallas kernels, body(): pl.pallas_call(functools.partial(snap_kernel, sizes), out_shape=(jax.Shap...  20.6 us
    pallas_call x1, Pallas kernels, body(): pl.pallas_call(functools.partial(basis_kernel, cells, planes), out_shape=...  3.28 us

profile of v2, /device:TPU:0, one launch (start us, length us, event | category | flops | bytes accessed | tf_op | source)
XLA Modules:
  0.0 23.9 jit_solution(11551726800912193090)
XLA Ops:
  0.0 20.6 %snap.1 = (bf16[64,16384]{1,0:T(8,128)(2,1)S(1)}, f32[8,128]{1,0:T(8,128)S(1)}) custom-call(f32[3,8,16,128]{3,2,1,0:T(8,128)} %f_ref.1, f32[3,8,16,128]{3,2,1,0:T(8,128)} %a_ref.1, f32[32,81]{1,0:T(8,128)} %w_ref.1), custom_call_target="tpu_custom_call" | custom-call | tf_op jit(solution)/shard_map/snap/pallas_call | solution.py:308
  20.6 3.3 %basis.1 = f32[32,8,16,128]{3,2,1,0:T(8,128)} custom-call(f32[8,128]{1,0:T(8,128)S(1)} %get-tuple-element.7.t_ref, bf16[64,16384]{1,0:T(8,128)(2,1)S(1)} %get-tuple-element.8.s_ref), custom_call_target="tpu_custom_call" | custom-call | tf_op jit(solution)/shard_map/basis/pallas_call | solution.py:340

commit v3 on v2

--- a/solution.py
+++ b/solution.py
@@ -23,7 +23,7 @@
 
 
 def snap_kernel(sizes, f_ref, a_ref, w_ref, s_ref, t_ref, px, py, hy, hz, ysend, zsend, wv, gs, sx, sz, lhs, acc,
-                one, two, local, send, recv, send1, recv1, send2, recv2):
+                one, two, relay, local, send, recv, send1, recv1, send2, recv2):
     n_s, n_y, n_z = sizes
     i_s, i_y, i_z = [lax.axis_index(name) for name in AXES]
     count = n_s * n_y
@@ -45,7 +45,7 @@
     greeted = 0
     for z in range(n_z):
         for k in range(count):
-            if (k or z) and (direct or not k or not z):
+            if (k or z) and (not k or not z):
                 peer = {**plane_peer(k), **depth_peer(z)}
                 pl.semaphore_signal(barrier, inc=1, device_id=peer, device_id_type=MESH)
                 greeted += 1
@@ -64,6 +64,8 @@
         load(ref, px.at[3 * k:3 * k + 3, 2:planes + 2])
     load(w_ref, wv)
     pl.semaphore_wait(barrier, greeted)
+    for k in range(1, n_z):
+        pl.semaphore_signal(relay, inc=1, device_id=depth_peer(k), device_id_type=MESH)
     copies = []
 
     def push(src, dst, peer):
@@ -221,6 +223,7 @@
             total = total + buf[k]
         return total
 
+    pl.semaphore_wait(relay, n_z - 1)
     if not direct:
         one[me] = packed
         two[i_z] = exchange(one, me, count, plane_peer, send1, recv1)
@@ -285,13 +288,11 @@
     left = jnp.concatenate(
         [jnp.concatenate([high, high], axis=1), jnp.concatenate([low, low], axis=1)], axis=0)
     rows = o_ref.shape[2]
-    flat = stage.reshape(32 * planes * rows, 128)
     copies = []
     for x in range(planes):
         wide = jnp.dot(left, s_ref[:, x * width:(x + 1) * width], preferred_element_type=F32)
         block = wide[:32] + wide[32:]
-        for y in range(rows):
-            flat[pl.ds(x * rows + y, 32, stride=planes * rows), :] = block[:, 128 * y:128 * y + 128]
+        stage[:, x * rows:(x + 1) * rows, :] = block.reshape(32, rows, 128)
         copy = pltpu.make_async_copy(stage.at[:, pl.ds(x * rows, rows), :], o_ref.at[:, x], sems.at[x])
         copy.start(priority=x % 2)
         copies.append(copy)
@@ -327,6 +328,7 @@
             pltpu.VMEM((64, 64), F32),
             pltpu.VMEM((slots, 8, 128), F32),
             pltpu.VMEM((sizes[2], 8, 128), F32),
+            pltpu.SemaphoreType.REGULAR,
             pltpu.SemaphoreType.DMA((9,)),
             pltpu.SemaphoreType.DMA((8,)),
             pltpu.SemaphoreType.DMA((8,)),

time: 24 us -> 23.2 us (0.967)
  Pallas kernels: 23.9 us -> 23 us
    pallas_call x1, Pallas kernels: 3.28 us -> 2.5 us  [body(): pl.pallas_call(functools.partial(basis_kernel, cells, planes), out_shape=...]
where the time goes in v3:
time: 23.2 us; the launch traced here: 23 us
  Pallas kernels  23 us (99%)
    pallas_call x1, Pallas kernels, body(): pl.pallas_call(functools.partial(snap_kernel, sizes), out_shape=(jax.Shap...  20.5 us
    pallas_call x1, Pallas kernels, body(): pl.pallas_call(functools.partial(basis_kernel, cells, planes), out_shape=...  2.5 us

profile of v3, /device:TPU:0, one launch (start us, length us, event | category | flops | bytes accessed | tf_op | source)
XLA Modules:
  0.0 23.0 jit_solution(15678542344221291830)
XLA Ops:
  0.0 20.5 %snap.1 = (bf16[64,16384]{1,0:T(8,128)(2,1)S(1)}, f32[8,128]{1,0:T(8,128)S(1)}) custom-call(f32[3,8,16,128]{3,2,1,0:T(8,128)} %f_ref.1, f32[3,8,16,128]{3,2,1,0:T(8,128)} %a_ref.1, f32[32,81]{1,0:T(8,128)} %w_ref.1), custom_call_target="tpu_custom_call" | custom-call | tf_op jit(solution)/shard_map/snap/pallas_call | solution.py:309
  20.5 2.5 %basis.1 = f32[32,8,16,128]{3,2,1,0:T(8,128)} custom-call(f32[8,128]{1,0:T(8,128)S(1)} %get-tuple-element.7.t_ref, bf16[64,16384]{1,0:T(8,128)(2,1)S(1)} %get-tuple-element.8.s_ref), custom_call_target="tpu_custom_call" | custom-call | tf_op jit(solution)/shard_map/basis/pallas_call | solution.py:342

commit v4 on v3

--- a/solution.py
+++ b/solution.py
@@ -154,6 +154,7 @@
 
     def plane(x, slot, ready):
         for k in range(2):
+            slopes = []
             halo_z = jnp.where(lane % 4 < 2, hz[1, k], hz[0, k])
             for c in range(3):
                 i = (3 * k + c) * planes + x
@@ -161,24 +162,25 @@
                 dy = stencil(*[py[i, 8 + o:8 + o + rows, :] for o in (-2, -1, 1, 2)])
                 edge = pltpu.roll(halo_z, lax.rem(254 - 4 * (c * planes + x), 128), 1)
                 dz = sz[i] + jnp.where((lane < 2) | (lane >= 126), edge, 0.0)
-                for d, slope in enumerate((dx, dy, dz)):
-                    gs[slot, pl.ds(16 * k + 3 * c + d, rows, stride=32), :] = slope
+                slopes += [dx, dy, dz]
+            gs[slot, 16 * k:16 * k + 8, :] = jnp.stack(slopes[:8]).reshape(8, cells)
+            gs[slot, 16 * k + 8:16 * k + 9, :] = slopes[8].reshape(1, cells)
         parts = []
         for pair in range(0, rows, 2):
             tiles = []
             for y in (pair, pair + 1):
-                base = 32 * y
-                f8 = gs[slot, base:base + 8, :]
-                a8 = gs[slot, base + 16:base + 24, :]
-                a_end = gs[slot, base + 24:base + 25, :]
+                at = slice(128 * y, 128 * y + 128)
+                f8 = gs[slot, 0:8, at]
+                a8 = gs[slot, 16:24, at]
+                a_end = gs[slot, 24:25, at]
                 blocks = []
                 for n in range(11):
                     if n < 9:
-                        part = gs[slot, base + n:base + n + 1, :] * a8
+                        part = gs[slot, n:n + 1, at] * a8
                     elif n == 9:
                         part = f8 * a_end
                     else:
-                        part = jnp.broadcast_to(gs[slot, base + 8:base + 9, :] * a_end, (8, 128))
+                        part = jnp.broadcast_to(gs[slot, 8:9, at] * a_end, (8, 128))
                     high = part.astype(BF16).astype(F32)
                     blocks.append(jnp.concatenate([high, part - high], axis=0).astype(BF16))
                 tiles.append(jnp.concatenate(blocks, axis=0))
@@ -321,7 +323,7 @@
             pltpu.VMEM((2, 2, 2 * half, depth), F32),
             pltpu.VMEM((2, 2, rows, depth), F32),
             pltpu.VMEM((32, 81), F32),
-            pltpu.VMEM((2, rows * 32, depth), F32),
+            pltpu.VMEM((2, 32, rows * depth), F32),
             pltpu.VMEM((2 * half, rows, depth), F32),
             pltpu.VMEM((2 * half, rows, depth), F32),
             pltpu.VMEM((64, 176), BF16),

time: 23.2 us -> 23.1 us (level)
  no operation moved by 1% of the time
where the time goes in v4:
time: 23.1 us; the launch traced here: 22.9 us
  Pallas kernels  22.9 us (99%)
    pallas_call x1, Pallas kernels, body(): pl.pallas_call(functools.partial(snap_kernel, sizes), out_shape=(jax.Shap...  20.4 us
    pallas_call x1, Pallas kernels, body(): pl.pallas_call(functools.partial(basis_kernel, cells, planes), out_shape=...  2.51 us

profile of v4, /device:TPU:0, one launch (start us, length us, event | category | flops | bytes accessed | tf_op | source)
XLA Modules:
  0.0 22.9 jit_solution(5475288080543086560)
XLA Ops:
  0.0 20.4 %snap.1 = (bf16[64,16384]{1,0:T(8,128)(2,1)S(1)}, f32[8,128]{1,0:T(8,128)S(1)}) custom-call(f32[3,8,16,128]{3,2,1,0:T(8,128)} %f_ref.1, f32[3,8,16,128]{3,2,1,0:T(8,128)} %a_ref.1, f32[32,81]{1,0:T(8,128)} %w_ref.1), custom_call_target="tpu_custom_call" | custom-call | tf_op jit(solution)/shard_map/snap/pallas_call | solution.py:311
  20.4 2.5 %basis.1 = f32[32,8,16,128]{3,2,1,0:T(8,128)} custom-call(f32[8,128]{1,0:T(8,128)S(1)} %get-tuple-element.7.t_ref, bf16[64,16384]{1,0:T(8,128)(2,1)S(1)} %get-tuple-element.8.s_ref), custom_call_target="tpu_custom_call" | custom-call | tf_op jit(solution)/shard_map/basis/pallas_call | solution.py:344
